TPU v7x, 32 devices: a whole 2x2x4 slice. The times are simulated.
32 devices in a mesh: row: 4 (over x, core), col: 8 (over z, y).
Axes of the slice: x: 2, y: 2, z: 4, core: 2. Of those that a mesh axis runs over, the one named last changes fastest.
Arguments:
- hidden_states: bfloat16 [4096, 3072], P(('row', 'col')), may hold values from -27 to 27
- norm_gain: float32 [3072], replicated, may hold values from 0.25 to 1.75
- gate_base: bfloat16 [3072, 8192], P('row', 'col'), may hold values from -0.109375 to 0.109375
- up_base: bfloat16 [3072, 8192], P('row', 'col'), may hold values from -0.109375 to 0.109375
- down_base: bfloat16 [8192, 3072], P('col', 'row'), may hold values from -0.0625 to 0.0625
- shrink_gu: bfloat16 [1024, 3072], P('col'), may hold values from -0.109375 to 0.109375
- expand_gu: bfloat16 [2, 512, 8192], P(None, None, 'col'), may hold values from -1.5 to 1.5
- down_shrink_maps: bfloat16 [512, 8192], P(None, 'col'), may hold values from -0.0625 to 0.0625
- down_expand_maps: bfloat16 [512, 3072], P('col'), may hold values from -1.5 to 1.5
- token_adapter: int32 [4096], P('row'), may hold values from 0 to 31, as said below
- adapter_slot: int32 [32], replicated, may hold values from 0 to 31, as said below
Outputs:
- mlp_out: bfloat16 [4096, 3072], P(('row', 'col'))
Inputs may be any that keep to these rules, and one draw needn't show every extreme that they name: `token_adapter`: split the tokens into aligned blocks of 128 and groups of 8 consecutive blocks: no block has more than 16 tokens whose adapters share one owner, and in each group one owner has exactly 16 tokens in every block. `adapter_slot`: A permutation of the slots.
All inputs are finite; a program needn't handle non-finite values.
Results may differ from a plain program's by a relative error of at most 0.017.
Values may be sent and summed in bfloat16 or wider, within the bound.
A program may use at most 128 MiB of HBM per device.

v0:
```python
import jax
import jax.numpy as jnp
from jax import lax
from jax.sharding import PartitionSpec as P

eps = 1e-05


def contract_trailing(left, right):
    return lax.dot_general(
        left, right, (((left.ndim - 1,), (1,)), ((), ())), preferred_element_type=jnp.float32
    )


def rms_normed(states, norm_gain):
    values = states.astype(jnp.float32)
    scale_inv = lax.rsqrt(jnp.mean(values * values, axis=-1, keepdims=True) + eps)
    return (values * scale_inv * norm_gain).astype(jnp.bfloat16)


def spread_rank_rows(select_mask, factors):
    widened_rows = select_mask[:, :, None] * factors[:, None, :]
    return widened_rows.reshape(factors.shape[0], select_mask.shape[1] * factors.shape[1])


def dispatch_table(own_slots, column_count, slot_capacity, owner_partial):
    owners = own_slots // owner_partial
    matches = (owners[:, None] == jnp.arange(column_count, dtype=jnp.int32)[None, :]).astype(
        jnp.int32
    )
    earlier = jnp.cumsum(matches, axis=0) - matches
    position = jnp.sum(earlier * matches, axis=1)
    target = owners * slot_capacity + position
    return (
        target[:, None] == jnp.arange(column_count * slot_capacity, dtype=jnp.int32)[None, :]
    ).astype(jnp.int32)


def local(
    hidden_states,
    norm_gain,
    gate_base,
    up_base,
    down_base,
    shrink_gu,
    expand_gu,
    down_shrink_maps,
    down_expand_maps,
    token_adapter,
    adapter_slot,
):
    column_count = lax.axis_size("col")
    col_index = lax.axis_index("col")
    own_count = hidden_states.shape[0]
    adapter_list = adapter_slot.shape[0]
    owner_partial = adapter_list // column_count
    adapter_rank = down_expand_maps.shape[0] // owner_partial
    slot_capacity = own_count // 8
    first_slot = col_index * owner_partial
    owned_range = jnp.arange(owner_partial, dtype=jnp.int32)
    adapter_range = jnp.arange(adapter_list, dtype=jnp.int32)
    normed = rms_normed(hidden_states, norm_gain)
    matches = (token_adapter[:, None] == adapter_range[None, :]).astype(jnp.int32)
    row_slots = jnp.sum(matches * adapter_slot[None, :], axis=1)
    own_slots = lax.dynamic_slice_in_dim(row_slots, col_index * own_count, own_count)
    dispatch = dispatch_table(own_slots, column_count, slot_capacity, owner_partial)
    dispatch_bf = dispatch.astype(jnp.bfloat16)
    sent_slots = (jnp.sum(dispatch * (own_slots[:, None] + 1), axis=0) - 1).reshape(
        column_count, slot_capacity
    )
    sent_slots_bf = sent_slots.astype(jnp.bfloat16)
    first_float = first_slot.astype(jnp.float32)
    owned_float = owned_range.astype(jnp.float32)
    sent_rows = jnp.dot(dispatch_bf.T, normed, preferred_element_type=jnp.float32).astype(
        jnp.bfloat16
    )
    sent_rows = sent_rows.reshape(column_count, slot_capacity, normed.shape[1])
    incoming_rows = lax.all_to_all(sent_rows, "col", split_axis=0, concat_axis=0, tiled=True)
    slots_in = lax.all_to_all(sent_slots_bf, "col", split_axis=0, concat_axis=0, tiled=True)
    local_slot = slots_in.astype(jnp.float32) - first_float
    select_mask = (local_slot[..., None] == owned_float).astype(jnp.float32)
    projected_rows = contract_trailing(incoming_rows, shrink_gu)
    projected_rows = projected_rows.reshape(
        incoming_rows.shape[0], incoming_rows.shape[1], owner_partial, 2 * adapter_rank
    )
    rank_values = jnp.sum(projected_rows * select_mask[..., None], axis=2).astype(jnp.bfloat16)
    returned_values = lax.all_to_all(rank_values, "col", split_axis=0, concat_axis=0, tiled=True)
    own_ranks = jnp.dot(
        dispatch_bf,
        returned_values.reshape(column_count * slot_capacity, 2 * adapter_rank),
        preferred_element_type=jnp.float32,
    ).astype(jnp.bfloat16)
    row_normed, rank_per_row = (
        lax.all_gather(normed, "col", axis=0, tiled=True),
        lax.all_gather(own_ranks, "col", axis=0, tiled=True),
    )
    total_row_count = row_normed.shape[0]
    gate_sum = jnp.dot(
        row_normed,
        lax.all_gather(gate_base, "row", axis=0, tiled=True),
        preferred_element_type=jnp.float32,
    )
    up_sum = jnp.dot(
        row_normed,
        lax.all_gather(up_base, "row", axis=0, tiled=True),
        preferred_element_type=jnp.float32,
    )
    row_selector = (row_slots[:, None] == adapter_range[None, :]).astype(jnp.bfloat16)
    gate_sum = gate_sum + jnp.dot(
        spread_rank_rows(row_selector, rank_per_row[:, :adapter_rank]),
        expand_gu[0],
        preferred_element_type=jnp.float32,
    )
    up_sum = up_sum + jnp.dot(
        spread_rank_rows(row_selector, rank_per_row[:, adapter_rank:]),
        expand_gu[1],
        preferred_element_type=jnp.float32,
    )
    hidden_rows = (jax.nn.silu(gate_sum) * up_sum).astype(jnp.bfloat16)
    down_projector = contract_trailing(hidden_rows, down_shrink_maps).reshape(
        total_row_count, adapter_list, adapter_rank
    )
    down_part = jnp.sum(down_projector * row_selector.astype(jnp.float32)[:, :, None], axis=1)
    down_ranks = lax.psum_scatter(
        down_part.astype(jnp.bfloat16), "col", scatter_dimension=0, tiled=True
    )
    down_full = lax.all_gather(down_base, "row", axis=1, tiled=True)
    down_total_sum = lax.psum_scatter(
        jnp.dot(hidden_rows, down_full, preferred_element_type=jnp.float32).astype(jnp.bfloat16),
        "col",
        scatter_dimension=0,
        tiled=True,
    ).astype(jnp.float32)
    outgoing_ranks = jnp.dot(dispatch_bf.T, down_ranks, preferred_element_type=jnp.float32).astype(
        jnp.bfloat16
    )
    outgoing_ranks = outgoing_ranks.reshape(column_count, slot_capacity, adapter_rank)
    incoming_ranks = lax.all_to_all(outgoing_ranks, "col", split_axis=0, concat_axis=0, tiled=True)
    slots_in = lax.all_to_all(sent_slots_bf, "col", split_axis=0, concat_axis=0, tiled=True)
    local_slot = slots_in.astype(jnp.float32) - first_float
    select_mask = (local_slot[..., None] == owned_float).astype(jnp.bfloat16)
    widened_rows = select_mask[..., None] * incoming_ranks[..., None, :]
    widened_rows = widened_rows.reshape(
        incoming_ranks.shape[0], incoming_ranks.shape[1], owner_partial * adapter_rank
    )
    rows_out = contract_trailing(widened_rows, jnp.transpose(down_expand_maps)).astype(jnp.bfloat16)
    returned_rows = lax.all_to_all(rows_out, "col", split_axis=0, concat_axis=0, tiled=True)
    adapter_down_term = jnp.dot(
        dispatch_bf,
        returned_rows.reshape(column_count * slot_capacity, returned_rows.shape[2]),
        preferred_element_type=jnp.float32,
    )
    return (down_total_sum + adapter_down_term).astype(jnp.bfloat16)


def solution(mesh):
    in_specs = (
        P(("row", "col"), None),
        P(),
        P("row", "col"),
        P("row", "col"),
        P("col", "row"),
        P("col", None),
        P(None, None, "col"),
        P(None, "col"),
        P("col", None),
        P("row"),
        P(),
    )
    out_specs = P(("row", "col"), None)
    return jax.shard_map(local, mesh=mesh, in_specs=in_specs, out_specs=out_specs, check_vma=False)
```

profile of v0, /device:TPU:0, one launch (start us, length us, event | category | flops | bytes accessed | tf_op | source)
XLA Modules:
  0.0 465.8 jit_solution(17228047332145046880)
XLA Ops:
  6.5 0.0 copy-start
  6.5 0.0 all-gather.9.cloned.1.call-start
  6.5 0.7 all-gather.9.cloned.1.call-update
  7.3 0.0 all-gather.5.cloned.1.call-start
  7.3 1.4 fusion.1
  8.7 2.4 fusion.3
  11.1 0.0 all-gather.5.cloned.1.call-update
  11.1 0.0 all-gather.7.cloned.1.call-start
  11.1 0.7 all-gather.7.cloned.1.call-update
  11.8 0.0 all-gather.11.cloned.1.call-start
  11.9 0.5 all-gather.11.cloned.1.call-update
  12.4 0.1 select_reduce_fusion
  12.5 0.1 broadcast_add_fusion
  12.6 0.1 fusion.13
  12.7 0.2 reduce_window_sum.11
  12.9 0.2 select_reduce_fusion.2
  13.1 0.1 select_reduce_fusion.1
  13.2 0.7 convert_element_type.133
  13.9 7.3 %all-to-all-start.1 = ((bf16[8,1,16]{2,1,0:T(2,128)(2,1)}), bf16[8,1,16]{2,1,0:T(2,128)(2,1)S(1)}, u32[]{:S(2)}, u32[]{:S(2)}) async-start(bf16[8,1,16]{2,1,0:T(2,128)(2,1)} %convert_element_type.133), calls=%async_computation.1 | async-start | bytes 8192 | tf_op jit(solution)/shard_map/all_to_all | solution.py:79
  21.2 1.4 convolution_convert_fusion.2
  22.6 5.0 %all-to-all-done.1 = bf16[8,1,16]{2,1,0:T(2,128)(2,1)S(1)} async-done(((bf16[8,1,16]{2,1,0:T(2,128)(2,1)}), bf16[8,1,16]{2,1,0:T(2,128)(2,1)S(1)}, u32[]{:S(2)}, u32[]{:S(2)}) %all-to-all-start.1) | async-done | bytes 288 | tf_op jit(solution)/shard_map/all_to_all | solution.py:79
  27.6 3.5 all-to-all-start
  31.2 0.1 compare_convert_fusion
  31.3 18.9 %all-to-all-done = bf16[8,16,3072]{2,1,0:T(8,128)(2,1)S(1)} async-done(((bf16[8,16,3072]{2,1,0:T(8,128)(2,1)}), bf16[8,16,3072]{2,1,0:T(8,128)(2,1)S(1)}, u32[]{:S(2)}, u32[]{:S(2)}) %all-to-all-start) | async-done | bytes 786464 | tf_op jit(solution)/shard_map/all_to_all | solution.py:78
  50.2 0.4 fusion.9
  50.6 0.2 reshape.143
  50.7 0.3 multiply_reduce_fusion.1
  51.0 0.7 reshape.152
  51.7 3.5 all-to-all-start.2
  55.2 0.0 reduce-scatter.7.cloned.1.call-start
  55.3 6.4 %all-to-all-done.2 = bf16[8,2,256]{2,1,0:T(2,128)(2,1)S(1)} async-done(((bf16[8,2,256]{2,1,0:T(2,128)(2,1)}), bf16[8,2,256]{2,1,0:T(2,128)(2,1)S(1)}, u32[]{:S(2)}, u32[]{:S(2)}) %all-to-all-start.2) | async-done | bytes 8224 | tf_op jit(solution)/shard_map/all_to_all | solution.py:87
  61.7 0.1 reshape.153
  61.8 0.2 convolution_convert_fusion.3
  62.0 26.7 %all_gather.17 = bf16[1024,32]{0,1:T(8,128)(2,1)S(1)} all-gather(bf16[128,32]{0,1:T(8,128)(2,1)S(1)} %convolution_convert_fusion.3), channel_id=1, replica_groups=mesh['row'=4,'col'=8] {'col'}, dimensions={0}, use_global_device_ids=true | all-gather | bytes 73728 | tf_op jit(solution)/shard_map/all_gather | solution.py:95
  88.8 0.1 broadcast_multiply_fusion
  88.9 4.4 fusion.5
  93.4 66.6 %all-gather.5.cloned.1.call-done = bf16[1024,3072]{1,0:T(8,128)(2,1)} async-done(((bf16[128,3072]{1,0:T(8,128)(2,1)}), bf16[1024,3072]{1,0:T(8,128)(2,1)}) %all-gather.5.cloned.1.call-update) | async-done | bytes 6291472 | tf_op jit(solution)/shard_map/all_gather | solution.py:94
  160.0 12.0 %fusion.21 = f32[1024,1024]{1,0:T(8,128)} fusion(bf16[1024,3072]{1,0:T(8,128)(2,1)} %all-gather.5.cloned.1.call-done, bf16[3072,1024]{1,0:T(8,128)(2,1)} %all-gather.9.cloned.1.call-done), kind=kOutput, calls=%fused_computation.56 | convolution fusion | flops 6442450944 | bytes 16777216 | tf_op jit(solution)/shard_map/dot_general | solution.py:103
  172.0 34.2 %all-gather.7.cloned.1.call-done = bf16[3072,1024]{1,0:T(8,128)(2,1)} async-done(((bf16[768,1024]{1,0:T(8,128)(2,1)}), bf16[3072,1024]{1,0:T(8,128)(2,1)}) %all-gather.7.cloned.1.call-update) | async-done | bytes 6291472 | tf_op jit(solution)/shard_map/all_gather | solution.py:100
  206.2 10.7 %fusion.20 = f32[1024,1024]{1,0:T(8,128)S(1)} fusion(bf16[1024,3072]{1,0:T(8,128)(2,1)} %all-gather.5.cloned.1.call-done, bf16[3072,1024]{1,0:T(8,128)(2,1)} %all-gather.7.cloned.1.call-done), kind=kOutput, calls=%fused_computation.55 | convolution fusion | flops 6442450944 | bytes 16777216 | tf_op jit(solution)/shard_map/dot_general | solution.py:98
  216.9 2.2 multiply_convert_fusion
  219.1 1.3 fusion.22
  220.5 0.0 copy-done.8
  220.5 0.3 multiply_reduce_fusion
  220.8 0.8 copy.29
  221.6 0.0 reduce-scatter.7.cloned.1.call-update
  221.6 0.2 reduce-scatter.5.cloned.1.call-start
  221.9 32.1 %all-gather.11.cloned.1.call-done = bf16[1024,3072]{1,0:T(8,128)(2,1)} async-done(((bf16[1024,768]{1,0:T(8,128)(2,1)}), bf16[1024,3072]{1,0:T(8,128)(2,1)}) %all-gather.11.cloned.1.call-update) | async-done | bytes 6291472 | tf_op jit(solution)/shard_map/all_gather | solution.py:127
  254.0 11.1 %convolution_convert_fusion = bf16[1024,3072]{1,0:T(8,128)(2,1)} fusion(bf16[1024,1024]{1,0:T(8,128)(2,1)} %copy-done.8, bf16[1024,3072]{1,0:T(8,128)(2,1)} %all-gather.11.cloned.1.call-done), kind=kOutput, calls=%fused_computation | convolution fusion | flops 6445596672 | bytes 14680064 | tf_op jit(solution)/shard_map/dot_general | solution.py:129
  265.0 0.0 reduce-scatter.5.cloned.1.call-update
  265.1 53.8 %reduce-scatter.7.cloned.1.call-done = bf16[128,16]{1,0:T(8,128)(2,1)} async-done(((bf16[1024,16]{1,0:T(8,128)(2,1)}), bf16[128,16]{1,0:T(8,128)(2,1)}) %reduce-scatter.7.cloned.1.call-update) | async-done | bytes 4112
  318.9 1.0 convolution_convert_fusion.4
  319.8 0.1 reshape.146
  319.9 0.1 reshape.154
  320.0 9.9 %all_to_all.27 = bf16[8,2,128]{2,1,0:T(2,128)(2,1)S(1)} all-to-all(bf16[8,2,128]{2,1,0:T(2,128)(2,1)S(1)} %reshape.154), channel_id=1, replica_groups=mesh['row'=4,'col'=8] {'col'}, dimensions={0} | all-to-all | bytes 8192 | tf_op jit(solution)/shard_map/all_to_all | solution.py:138
  329.9 0.1 reshape.155
  330.0 0.1 copy.28
  330.1 0.2 broadcast_multiply_fusion.2
  330.3 0.1 mul.164
  330.4 0.0 copy-done.5
  330.4 0.3 convolution_convert_fusion.1
  330.8 42.4 %all_to_all.28 = bf16[8,16,3072]{2,1,0:T(8,128)(2,1)S(1)} all-to-all(bf16[8,16,3072]{2,1,0:T(8,128)(2,1)S(1)} %convolution_convert_fusion.1), channel_id=1, replica_groups=mesh['row'=4,'col'=8] {'col'}, dimensions={0} | all-to-all | bytes 1572864 | tf_op jit(solution)/shard_map/all_to_all | solution.py:147
  373.2 83.4 %reduce-scatter.5.cloned.1.call-done = bf16[128,3072]{1,0:T(8,128)(2,1)} async-done(((bf16[1024,3072]{1,0:T(8,128)(2,1)}), bf16[128,3072]{1,0:T(8,128)(2,1)}) %reduce-scatter.5.cloned.1.call-update) | async-done | bytes 786448 | tf_op jit(solution)/shard_map/reduce_scatter | solution.py:128
  456.5 2.4 fusion
  (26 shorter events, 0.1 us)
Async XLA Ops:
  6.5 212.6 %copy-start = (bf16[512,1024]{1,0:T(8,128)(2,1)S(1)}, bf16[512,1024]{1,0:T(8,128)(2,1)}, u32[]{:S(2)}) copy-start(bf16[512,1024]{1,0:T(8,128)(2,1)} %param.18) | copy-start | bytes 3145732
  6.5 5.9 %copy-start.7 = (s32[32]{0:T(128)S(1)}, s32[32]{0:T(128)}, u32[]{:S(2)}) copy-start(s32[32]{0:T(128)} %param.21) | copy-start | bytes 388
  6.5 5.9 %copy-start.6 = (s32[1024]{0:T(1024)S(1)}, s32[1024]{0:T(1024)}, u32[]{:S(2)}) copy-start(s32[1024]{0:T(1024)} %param.20) | copy-start | bytes 12292
  6.5 86.8 %all-gather.9.cloned.1.call-start = ((), (), s32[]{:S(2)}) async-start(), calls=%async_computation.9 | async-start | bytes 7864320 | tf_op jit(solution)/shard_map/all_gather | solution.py:105
  7.3 152.7 %all-gather.5.cloned.1.call-start = ((), (), s32[]{:S(2)}) async-start(), calls=%async_computation.7 | async-start | bytes 7077888 | tf_op jit(solution)/shard_map/all_gather | solution.py:94
  8.7 41.5 %copy-start.3 = (bf16[128,3072]{1,0:T(8,128)(2,1)S(1)}, bf16[128,3072]{1,0:T(8,128)(2,1)}, u32[]{:S(2)}) copy-start(bf16[128,3072]{1,0:T(8,128)(2,1)} %param.16) | copy-start | bytes 2359300
  11.1 10.1 %copy-start.1 = (bf16[128,3072]{1,0:T(8,128)(2,1)S(1)}, bf16[128,3072]{1,0:T(8,128)(2,1)}, u32[]{:S(2)}) copy-start(bf16[128,3072]{1,0:T(8,128)(2,1)} %fusion.3) | copy-start | bytes 2359300
  11.1 195.1 %all-gather.7.cloned.1.call-start = ((), (), s32[]{:S(2)}) async-start(), calls=%async_computation.8 | async-start | bytes 7864320 | tf_op jit(solution)/shard_map/all_gather | solution.py:100
  11.8 242.2 %all-gather.11.cloned.1.call-start = ((), (), s32[]{:S(2)}) async-start(), calls=%async_computation.10 | async-start | bytes 7864320 | tf_op jit(solution)/shard_map/all_gather | solution.py:127
  13.9 13.7 %all-to-all-start.1 = ((bf16[8,1,16]{2,1,0:T(2,128)(2,1)}), bf16[8,1,16]{2,1,0:T(2,128)(2,1)S(1)}, u32[]{:S(2)}, u32[]{:S(2)}) async-start(bf16[8,1,16]{2,1,0:T(2,128)(2,1)} %convert_element_type.133), calls=%async_computation.1 | async-start | bytes 8192 | tf_op jit(solution)/shard_map/all_to_all | solution.py:79
  27.6 22.6 %all-to-all-start = ((bf16[8,16,3072]{2,1,0:T(8,128)(2,1)}), bf16[8,16,3072]{2,1,0:T(8,128)(2,1)S(1)}, u32[]{:S(2)}, u32[]{:S(2)}) async-start(bf16[8,16,3072]{2,1,0:T(8,128)(2,1)} %bitcast), calls=%async_computation | async-start | bytes 1572864 | tf_op jit(solution)/shard_map/all_to_all | solution.py:78
  51.7 10.0 %all-to-all-start.2 = ((bf16[8,2,256]{2,1,0:T(2,128)(2,1)}), bf16[8,2,256]{2,1,0:T(2,128)(2,1)S(1)}, u32[]{:S(2)}, u32[]{:S(2)}) async-start(bf16[8,2,256]{2,1,0:T(2,128)(2,1)} %reshape.152), calls=%async_computation.2 | async-start | bytes 16384 | tf_op jit(solution)/shard_map/all_to_all | solution.py:87
  55.2 263.7 %reduce-scatter.7.cloned.1.call-start = ((), (), s32[]{:S(2)}) async-start(), calls=%async_computation.12 | async-start | bytes 294912
  206.2 10.7 %copy-start.2 = (f32[1024,1024]{1,0:T(8,128)S(1)}, f32[1024,1024]{1,0:T(8,128)}, u32[]{:S(2)}) copy-start(f32[1024,1024]{1,0:T(8,128)} %fusion.5) | copy-start | bytes 12582916
  206.2 10.7 %copy-start.4 = (bf16[2,512,1024]{2,1,0:T(8,128)(2,1)S(1)}, bf16[2,512,1024]{2,1,0:T(8,128)(2,1)}, u32[]{:S(2)}) copy-start(bf16[2,512,1024]{2,1,0:T(8,128)(2,1)} %param.17) | copy-start | bytes 6291460
  206.2 10.7 %copy-start.9 = (f32[1024,1024]{1,0:T(8,128)S(1)}, f32[1024,1024]{1,0:T(8,128)}, u32[]{:S(2)}) copy-start(f32[1024,1024]{1,0:T(8,128)} %fusion.21) | copy-start | bytes 12582916
  219.1 1.3 copy-start.8
  221.6 234.9 %reduce-scatter.5.cloned.1.call-start = ((), (), s32[]{:S(2)}) async-start(), calls=%async_computation.11 | async-start | bytes 7077888 | tf_op jit(solution)/shard_map/reduce_scatter | solution.py:128
  265.0 65.4 %copy-start.5 = (bf16[64,3072]{1,0:T(8,128)(2,1)S(1)}, bf16[64,3072]{1,0:T(8,128)(2,1)}, u32[]{:S(2)}) copy-start(bf16[64,3072]{1,0:T(8,128)(2,1)} %param.19) | copy-start | bytes 1179652
Sparse Core Ops, SparseCore 0:
  8.9 49.0 all-gather.8
  60.2 99.7 all-gather.4
  161.6 44.5 all-gather.6
  207.6 46.3 all-gather.10
  257.2 61.6 reduce-scatter.6
  322.3 134.1 reduce-scatter.4
where the time goes:
time: 466 us
  waiting for transfers between devices  302 us (65%)
  blocking collectives  79 us (17%)
  matrix products  47.4 us (10%)
  starting transfers between devices  14.7 us (3%)
  between operations  13.7 us (3%)
  other arithmetic  5.49 us (1%)
    reduce_scatter x1, waiting for transfers between devices, local(): lax.psum_scatter(jnp.dot(hidden_rows, down_full, preferred_element_type=j...  83.4 us
    all_gather x1, waiting for transfers between devices, local(): lax.all_gather(normed, 'col', axis=0, tiled=True)  66.6 us
    unnamed x7, waiting for transfers between devices  55.8 us
    all_to_all x1, blocking collectives, local(): lax.all_to_all(rows_out, 'col', split_axis=0, concat_axis=0, tiled=True)  42.4 us
    all_gather x1, waiting for transfers between devices, local(): lax.all_gather(gate_base, 'row', axis=0, tiled=True)  34.2 us
    all_gather x1, waiting for transfers between devices, local(): down_full = lax.all_gather(down_base, 'row', axis=1, tiled=True)  32.1 us
    all_gather x1, blocking collectives, local(): lax.all_gather(own_ranks, 'col', axis=0, tiled=True)  26.7 us
    all_to_all x1, waiting for transfers between devices, local(): lax.all_to_all(sent_rows, 'col', split_axis=0, concat_axis=0, tiled=True)  18.9 us
  transfers between devices with their start and end apart: 9, of which 8 were waited for; matrix products, arithmetic and copies ran while one was open for 11% of the time, Pallas kernels for 0%

commit v1 on v0

v1 whole, which is shorter than its diff:
```python
import functools

import jax
import jax.numpy as jnp
from jax import lax
from jax.experimental import pallas as pl
from jax.experimental.pallas import tpu as pltpu
from jax.sharding import PartitionSpec as P

eps = 1e-05
MESH = pl.DeviceIdType.MESH
VMEM_BYTES = 56 * 1024 * 1024


def contract_trailing(left, right):
    return lax.dot_general(
        left, right, (((left.ndim - 1,), (1,)), ((), ())), preferred_element_type=jnp.float32
    )


def rms_normed(states, norm_gain):
    values = states.astype(jnp.float32)
    scale_inv = lax.rsqrt(jnp.mean(values * values, axis=-1, keepdims=True) + eps)
    return (values * scale_inv * norm_gain).astype(jnp.bfloat16)


def ring_col(position, n):
    half = n // 2
    return jnp.where(position < half, 2 * position, 2 * (n - 1 - position) + 1)


def ring_position(col, n):
    return jnp.where(lax.rem(col, 2) == 0, col // 2, n - 1 - col // 2)


def wrap(value, n):
    return lax.rem(value + 2 * n, n)


def signal_all(devices):
    barrier = pltpu.get_barrier_semaphore()
    for device in devices:
        pl.semaphore_signal(barrier, inc=1, device_id=device, device_id_type=MESH)
    pl.semaphore_wait(barrier, len(devices))


def gather_kernel(
    n_row,
    n_col,
    tok,
    shr,
    dex,
    gate,
    up,
    down,
    tok_o,
    shr_o,
    dex_o,
    gate_o,
    up_o,
    down_o,
    own_sem,
    ring_send,
    ring_recv,
    core_send,
    core_recv,
    x_send,
    x_recv,
    pair_send,
    pair_recv,
):
    row, col = lax.axis_index("row"), lax.axis_index("col")
    n_x = n_row // 2
    x, core = row // 2, lax.rem(row, 2)
    here = ring_position(col, n_col)
    right = (row, ring_col(wrap(here + 1, n_col), n_col))
    left = (row, ring_col(wrap(here - 1, n_col), n_col))
    twin_row = x * 2 + 1 - core
    twin = (twin_row, col)
    x_peers = [(wrap(x + k, n_x) * 2 + core, col) for k in range(1, n_x)]
    signal_all([left, right, twin] + x_peers)

    t_rows, s_rows, e_rows = tok.shape[0], shr.shape[0], dex.shape[0]
    t_half, s_half, e_half = t_rows // 2, s_rows // 4, e_rows // 4

    def rows(ref, start, count):
        return ref.at[pl.ds(pl.multiple_of(start, 16), count), :]

    def place(a, block, d, c):
        if a == 0:
            return rows(tok_o, block * t_rows + d * t_half, t_half)
        if a == 1:
            base = c * (n_col * s_rows // 2) + block * (s_rows // 2)
            return rows(shr_o, base + d * s_half, s_half)
        return rows(dex_o, block * e_rows + (2 * c + d) * e_half, e_half)

    def first(a, d):
        if a == 0:
            return rows(tok, d * t_half, t_half)
        if a == 1:
            return rows(shr, core * (s_rows // 2) + d * s_half, s_half)
        return rows(dex, (2 * core + d) * e_half, e_half)

    def weight_place(w, r):
        if w == 2:
            width = down.shape[1]
            return down_o.at[:, pl.ds(pl.multiple_of(r * width, 128), width)]
        depth = gate.shape[0]
        return rows((gate_o, up_o)[w], r * depth, depth)

    weights = (gate, up, down)

    def x_copy(w, k, source, place_row):
        return pltpu.make_async_remote_copy(
            src_ref=source,
            dst_ref=weight_place(w, place_row),
            send_sem=x_send.at[w, k - 1],
            recv_sem=x_recv.at[w, k - 1],
            device_id=x_peers[k - 1],
            device_id_type=MESH,
        )

    def pair_copy(w, k, source, place_row):
        return pltpu.make_async_remote_copy(
            src_ref=source,
            dst_ref=weight_place(w, place_row),
            send_sem=pair_send.at[w, k],
            recv_sem=pair_recv.at[w, k],
            device_id=twin,
            device_id_type=MESH,
        )

    def ring_copy(a, d, step, source, block):
        return pltpu.make_async_remote_copy(
            src_ref=source,
            dst_ref=place(a, block, d, core),
            send_sem=ring_send.at[a, d, step],
            recv_sem=ring_recv.at[a, d, step],
            device_id=(right, left)[d],
            device_id_type=MESH,
        )

    def twin_copy(a, d, step, block, c):
        piece = place(a, block, d, c)
        return pltpu.make_async_remote_copy(
            src_ref=piece,
            dst_ref=piece,
            send_sem=core_send.at[a - 1, d, step],
            recv_sem=core_recv.at[a - 1, d, step],
            device_id=twin,
            device_id_type=MESH,
        )

    def block_of(d, step):
        sign = (1, -1)[d]
        return ring_col(wrap(here - sign * (1 + step), n_col), n_col)

    sides = (0, 1)
    arrays = (0, 1, 2)
    for a in arrays:
        for d in sides:
            ring_copy(a, d, 0, first(a, d), col).start()
    for w in range(3):
        for k in range(1, n_x):
            x_copy(w, k, weights[w], row).start()
    own = [
        pltpu.make_async_copy(tok, rows(tok_o, col * t_rows, t_rows), own_sem.at[0]),
        pltpu.make_async_copy(dex, rows(dex_o, col * e_rows, e_rows), own_sem.at[1]),
    ]
    for c in range(2):
        own.append(
            pltpu.make_async_copy(
                rows(shr, c * (s_rows // 2), s_rows // 2),
                rows(shr_o, (c * n_col + col) * (s_rows // 2), s_rows // 2),
                own_sem.at[2 + c],
            )
        )
    for w in range(3):
        pair_copy(w, 0, weights[w], row).start()
        own.append(pltpu.make_async_copy(weights[w], weight_place(w, row), own_sem.at[4 + w]))
    for copy in own:
        copy.start()

    last = n_col - 2

    def ring_step(step, forward):
        for a in arrays:
            for d in sides:
                block = block_of(d, step)
                piece = place(a, block, d, core)
                ring_copy(a, d, step, piece, block).wait_recv()
                if forward:
                    ring_copy(a, d, step + 1, piece, block).start()
                if a:
                    twin_copy(a, d, step, block, core).start()

    def steps(start, stop):
        @pl.loop(start, stop)
        def _(step):
            ring_step(step, True)

    def pass_on(w):
        for k in range(1, n_x):
            source_row = wrap(x - k, n_x) * 2 + core
            piece = weight_place(w, source_row)
            x_copy(w, k, piece, source_row).wait_recv()
            pair_copy(w, k, piece, source_row).start()

    steps(0, last // 2)
    pass_on(0)
    steps(last // 2, last)
    pass_on(1)
    ring_step(last, False)
    pass_on(2)

    @pl.loop(0, last + 1)
    def _(step):
        for a in arrays:
            for d in sides:
                block = block_of(d, step)
                ring_copy(a, d, step, place(a, block, d, core), block).wait_send()
                if a:
                    twin_copy(a, d, step, block, core).wait_send()
                    twin_copy(a, d, step, block, 1 - core).wait_recv()

    for w in range(3):
        for k in range(n_x):
            if k:
                x_copy(w, k, weights[w], row).wait_send()
            source_row = wrap(x - k, n_x) * 2 + core
            pair_copy(w, k, weight_place(w, source_row), source_row).wait_send()
            twin_source = wrap(x - k, n_x) * 2 + 1 - core
            pair_copy(w, k, weight_place(w, twin_source), twin_source).wait_recv()
    for copy in own:
        copy.wait()


def gather_all(n_row, n_col, tok, shr, dex, gate, up, down):
    bf = jnp.bfloat16
    outs = [
        (n_col * tok.shape[0], tok.shape[1]),
        (n_col * shr.shape[0], shr.shape[1]),
        (n_col * dex.shape[0], dex.shape[1]),
        (n_row * gate.shape[0], gate.shape[1]),
        (n_row * up.shape[0], up.shape[1]),
        (down.shape[0], n_row * down.shape[1]),
    ]
    n_x, steps = n_row // 2, n_col - 1
    dma = pltpu.SemaphoreType.DMA
    return pl.pallas_call(
        functools.partial(gather_kernel, n_row, n_col),
        out_shape=[jax.ShapeDtypeStruct(s, bf) for s in outs],
        in_specs=[pl.BlockSpec(memory_space=pl.ANY)] * 6,
        out_specs=[pl.BlockSpec(memory_space=pl.ANY)] * 6,
        scratch_shapes=[
            dma((7,)),
            dma((3, 2, steps)),
            dma((3, 2, steps)),
            dma((2, 2, steps)),
            dma((2, 2, steps)),
            dma((3, n_x - 1)),
            dma((3, n_x - 1)),
            dma((3, n_x)),
            dma((3, n_x)),
        ],
        compiler_params=pltpu.CompilerParams(
            collective_id=0, has_side_effects=True, vmem_limit_bytes=VMEM_BYTES
        ),
        name="gather_all",
    )(tok, shr, dex, gate, up, down)


def reduce_kernel(n_col, subs, part, out, held, send_sem, recv_sem):
    row, col = lax.axis_index("row"), lax.axis_index("col")
    here = ring_position(col, n_col)
    right = (row, ring_col(wrap(here + 1, n_col), n_col))
    left = (row, ring_col(wrap(here - 1, n_col), n_col))
    signal_all([left, right])
    own = out.shape[0]
    count = own // (2 * subs)
    streams = [(d, u) for u in range(subs) for d in range(2)]

    def offset(d, u):
        return (d * subs + u) * count

    def own_part(block, d, u):
        return part.at[pl.ds(pl.multiple_of(block * own + offset(d, u), 16), count), :]

    def target(d, step):
        sign = (1, -1)[d]
        return ring_col(wrap(here - sign * (2 + step), n_col), n_col)

    def copy(d, u, step, source):
        return pltpu.make_async_remote_copy(
            src_ref=source,
            dst_ref=held.at[d, u, step],
            send_sem=send_sem.at[d, u, step],
            recv_sem=recv_sem.at[d, u, step],
            device_id=(right, left)[d],
            device_id_type=MESH,
        )

    for d, u in streams:
        copy(d, u, 0, own_part((left, right)[d][1], d, u)).start()
    last = n_col - 2

    @pl.loop(0, last)
    def _(step):
        for d, u in streams:
            slot = held.at[d, u, step]
            copy(d, u, step, slot).wait_recv()
            total = slot[...].astype(jnp.float32) + own_part(target(d, step), d, u)[...].astype(
                jnp.float32
            )
            slot[...] = total.astype(jnp.bfloat16)
            copy(d, u, step + 1, slot).start()

    for d, u in streams:
        slot = held.at[d, u, last]
        copy(d, u, last, slot).wait_recv()
        total = slot[...].astype(jnp.float32) + own_part(col, d, u)[...].astype(jnp.float32)
        out[pl.ds(offset(d, u), count), :] = total.astype(jnp.bfloat16)

    @pl.loop(0, last + 1)
    def _(step):
        for d, u in streams:
            copy(d, u, step, held.at[d, u, step]).wait_send()


def reduce_blocks(n_col, part):
    own, width = part.shape[0] // n_col, part.shape[1]
    subs = 2
    steps = n_col - 1
    dma = pltpu.SemaphoreType.DMA
    return pl.pallas_call(
        functools.partial(reduce_kernel, n_col, subs),
        out_shape=jax.ShapeDtypeStruct((own, width), jnp.bfloat16),
        in_specs=[pl.BlockSpec(memory_space=pltpu.VMEM)],
        out_specs=pl.BlockSpec(memory_space=pltpu.VMEM),
        scratch_shapes=[
            pltpu.VMEM((2, subs, steps, own // (2 * subs), width), jnp.bfloat16),
            dma((2, subs, steps)),
            dma((2, subs, steps)),
        ],
        compiler_params=pltpu.CompilerParams(
            collective_id=1, has_side_effects=True, vmem_limit_bytes=VMEM_BYTES
        ),
        name="reduce_blocks",
    )(part)


def local(
    n_row,
    n_col,
    hidden_states,
    norm_gain,
    gate_base,
    up_base,
    down_base,
    shrink_gu,
    expand_gu,
    down_shrink_maps,
    down_expand_maps,
    token_adapter,
    adapter_slot,
):
    adapter_list = adapter_slot.shape[0]
    owned = adapter_list // n_col
    rank = down_expand_maps.shape[0] // owned
    adapter_range = jnp.arange(adapter_list, dtype=jnp.int32)
    normed = rms_normed(hidden_states, norm_gain)
    matches = (token_adapter[:, None] == adapter_range[None, :]).astype(jnp.int32)
    row_slots = jnp.sum(matches * adapter_slot[None, :], axis=1)
    by_side = (
        shrink_gu.reshape(owned, 2, rank, -1).transpose(1, 0, 2, 3).reshape(shrink_gu.shape)
    )
    tokens, shrink, expand_down, gate_full, up_full, down_full = gather_all(
        n_row, n_col, normed, by_side, down_expand_maps, gate_base, up_base, down_base
    )
    ranks = adapter_list * rank
    chosen = (jnp.arange(ranks, dtype=jnp.int32) // rank)[None, :] == row_slots[:, None]

    def spread(projected):
        return jnp.where(chosen, projected, 0.0).astype(jnp.bfloat16)

    def dot(left, right):
        return jnp.dot(left, right, preferred_element_type=jnp.float32)

    gate_sum = dot(tokens, gate_full) + dot(
        spread(contract_trailing(tokens, shrink[:ranks])), expand_gu[0]
    )
    up_sum = dot(tokens, up_full) + dot(
        spread(contract_trailing(tokens, shrink[ranks:])), expand_gu[1]
    )
    hidden_rows = (jax.nn.silu(gate_sum) * up_sum).astype(jnp.bfloat16)
    down_spread = spread(contract_trailing(hidden_rows, down_shrink_maps))
    part = (dot(hidden_rows, down_full) + dot(down_spread, expand_down)).astype(jnp.bfloat16)
    return reduce_blocks(n_col, part)


def solution(mesh):
    in_specs = (
        P(("row", "col"), None),
        P(),
        P("row", "col"),
        P("row", "col"),
        P("col", "row"),
        P("col", None),
        P(None, None, "col"),
        P(None, "col"),
        P("col", None),
        P("row"),
        P(),
    )
    out_specs = P(("row", "col"), None)
    return jax.shard_map(
        functools.partial(local, mesh.shape["row"], mesh.shape["col"]),
        mesh=mesh,
        in_specs=in_specs,
        out_specs=out_specs,
        check_vma=False,
    )
```

time: 466 us -> 351 us (0.75)
  waiting for transfers between devices: 302 us -> 0 us
  Pallas kernels: 0 us -> 275 us
  blocking collectives: 79 us -> 0 us
  matrix products: 47.4 us -> 67.7 us
  starting transfers between devices: 14.7 us -> 0 us
  between operations: 13.7 us -> 0.08 us
    pallas_call x0 -> x2, Pallas kernels: none -> 275 us  [the longest x1 208 us: gather_all(): pl.pallas_call(functools.partial(gather_kernel, n_row, n_col), out_shape=...]
    all_gather x4 -> x0, waiting for transfers between devices: 133 us -> none  [the longest x1 66.6 us: local(): lax.all_gather(normed, 'col', axis=0, tiled=True)]
    reduce_scatter x1 -> x0, waiting for transfers between devices: 83.4 us -> none  [local(): lax.psum_scatter(jnp.dot(hidden_rows, down_full, preferred_element_type=j...]
    unnamed x7 -> x0, waiting for transfers between devices: 55.8 us -> none
    all_to_all x2 -> x0, blocking collectives: 52.2 us -> none  [the longest x1 42.4 us: local(): lax.all_to_all(rows_out, 'col', split_axis=0, concat_axis=0, tiled=True)]
    all_to_all x3 -> x0, waiting for transfers between devices: 30.4 us -> none  [the longest x1 18.9 us: local(): lax.all_to_all(sent_rows, 'col', split_axis=0, concat_axis=0, tiled=True)]
    all_gather x1 -> x0, blocking collectives: 26.7 us -> none  [local(): lax.all_gather(own_ranks, 'col', axis=0, tiled=True)]
    dot_general x12 -> x6, matrix products: 47.4 us -> 67.7 us  [dot(): return jnp.dot(left, right, preferred_element_type=jnp.float32)]
  transfers between devices with their start and end apart: 9 -> 0, of which waited for: 8 -> 0; matrix products, arithmetic and copies ran while one was open for 11% -> 0% of each run, Pallas kernels for 0% -> 0%
where the time goes in v1:
time: 351 us; the launch traced here: 350 us
  Pallas kernels  275 us (78%)
  matrix products  67.7 us (19%)
  local copies, waits for them, and re-layouts  4.17 us (1%)
  other arithmetic  3.85 us (1%)
    pallas_call x1, Pallas kernels, gather_all(): pl.pallas_call(functools.partial(gather_kernel, n_row, n_col), out_shape=...  208 us
    dot_general x6, matrix products, dot(): return jnp.dot(left, right, preferred_element_type=jnp.float32)  67.7 us
    pallas_call x1, Pallas kernels, reduce_blocks(): pl.pallas_call(functools.partial(reduce_kernel, n_col, subs), out_shape=j...  66.6 us

profile of v1, /device:TPU:0, one launch (start us, length us, event | category | flops | bytes accessed | tf_op | source)
XLA Modules:
  0.0 350.5 jit_solution(7531493797300862648)
XLA Ops:
  0.0 0.0 copy-start
  0.0 1.5 fusion.11
  1.5 2.3 fusion.13.tok
  3.8 2.1 copy.13
  5.8 208.1 %gather_all.1 = (bf16[1024,3072]{1,0:T(8,128)(2,1)}, bf16[1024,3072]{1,0:T(8,128)(2,1)}, bf16[512,3072]{1,0:T(8,128)(2,1)}, bf16[3072,1024]{1,0:T(8,128)(2,1)}, ...) custom-call(bf16[128,3072]{1,0:T(8,128)(2,1)} %fusion.13.tok, bf16[128,3072]{1,0:T(8,128)(2,1)} %bitcast.21, ...), custom_call_target="tpu_custom_call" | custom-call | tf_op jit(solution)/shard_map/gather_all/pallas_call | solution.py:250
  213.9 0.0 copy-start.3
  213.9 0.0 copy-start.4
  214.0 12.1 %fusion.33 = f32[1024,1024]{1,0:T(8,128)} fusion(bf16[1024,3072]{1,0:T(8,128)(2,1)} %get-tuple-element.11, bf16[3072,1024]{1,0:T(8,128)(2,1)} %get-tuple-element.14), kind=kOutput, calls=%fused_computation.39 | convolution fusion | flops 6442450944 | bytes 16777216 | tf_op jit(solution)/shard_map/dot_general | solution.py:387
  226.0 0.0 copy-done.3
  226.0 0.0 copy-done.4
  226.0 0.0 copy-start.1
  226.1 0.0 copy-start.2
  226.1 0.0 copy-start.5
  226.1 8.3 %fusion.32 = f32[1024,1024]{1,0:T(8,128)} fusion(bf16[1024,3072]{1,0:T(8,128)(2,1)S(1)} %copy-done.3, bf16[3072,1024]{1,0:T(8,128)(2,1)S(1)} %copy-done.4), kind=kOutput, calls=%fused_computation.38 | convolution fusion | flops 6442450944 | bytes 16777216 | tf_op jit(solution)/shard_map/dot_general | solution.py:387
  234.3 0.0 copy-done.1
  234.3 0.0 copy-done.2
  234.3 0.1 select_reduce_fusion
  234.4 0.0 copy-done.5
  234.4 10.3 %fusion.17 = f32[1024,1024]{1,0:T(8,128)} fusion(bf16[2,512,1024]{2,1,0:T(8,128)(2,1)S(1)} %copy-done.5, bf16[1024,3072]{1,0:T(8,128)(2,1)} %get-tuple-element.11, bf16[1024,3072]{1,0:T(8,128)(2,1)} %get-tuple-element.13, s32[512]{0:T(512)S(1)} %add_select_fusion, s32[1024]{0:T(1024)S(1)} %select_reduce_fusion), kind=kOutput, calls=%fused_computation.18 | convolution fusion | flops 4296540160 | bytes 14686208 | tf_op jit(solution)/shard_map/dot_general | solution.py:387
  244.7 13.7 %multiply_convert_fusion = bf16[1024,1024]{1,0:T(8,128)(2,1)} fusion(f32[1024,1024]{1,0:T(8,128)} %fusion.33, f32[1024,1024]{1,0:T(8,128)} %fusion.32, f32[1024,1024]{1,0:T(8,128)} %fusion.17, bf16[1024,3072]{1,0:T(8,128)(2,1)} %get-tuple-element.11, bf16[1024,3072]{1,0:T(8,128)(2,1)} %get-tuple-element.13, bf16[2,512,1024]{2,1,0:T(8,128)(2,1)S(1)} %copy-done.5, ...), kind=kOutput, calls=%fused_computation.1 | convolution fusion | flops 4304928768 | bytes 25171968 | tf_op jit(solution)/shard_map/dot_general | solution.py:387
  258.4 0.0 copy-start.6
  258.4 13.0 %fusion.34 = f32[1024,3072]{1,0:T(8,128)} fusion(bf16[1024,1024]{1,0:T(8,128)(2,1)} %multiply_convert_fusion, bf16[1024,3072]{1,0:T(8,128)(2,1)} %get-tuple-element.15), kind=kOutput, calls=%fused_computation.40 | convolution fusion | flops 6442450944 | bytes 20971520 | tf_op jit(solution)/shard_map/dot_general | solution.py:387
  271.4 0.0 copy-done
  271.4 0.0 copy-done.6
  271.4 10.5 %add_convert_fusion.part = bf16[1024,3072]{1,0:T(8,128)(2,1)} fusion(f32[1024,3072]{1,0:T(8,128)} %fusion.34, bf16[512,3072]{1,0:T(8,128)(2,1)} %get-tuple-element.16, bf16[1024,1024]{1,0:T(8,128)(2,1)S(1)} %copy-done.6, bf16[512,1024]{1,0:T(8,128)(2,1)S(1)} %copy-done, s32[512]{0:T(512)S(1)} %add_select_fusion, s32[1024]{0:T(1024)S(1)} %select_reduce_fusion), kind=kOutput, calls=%fused_computation | convolution fusion | flops 4302831616 | bytes 25171968 | tf_op jit(solution)/shard_map/dot_general | solution.py:387
  281.8 66.6 %reduce_blocks.1 = bf16[128,3072]{1,0:T(8,128)(2,1)} custom-call(bf16[1024,3072]{1,0:T(8,128)(2,1)} %add_convert_fusion.part), custom_call_target="tpu_custom_call" | custom-call | tf_op jit(solution)/shard_map/reduce_blocks/pallas_call | solution.py:335
  348.4 2.1 copy.15
  (2 shorter events, 0.0 us)
Async XLA Ops:
  0.0 271.4 %copy-start = (bf16[512,1024]{1,0:T(8,128)(2,1)S(1)}, bf16[512,1024]{1,0:T(8,128)(2,1)}, u32[]{:S(2)}) copy-start(bf16[512,1024]{1,0:T(8,128)(2,1)} %param.18) | copy-start | bytes 3145732
  213.9 12.1 %copy-start.3 = (bf16[1024,3072]{1,0:T(8,128)(2,1)S(1)}, bf16[1024,3072]{1,0:T(8,128)(2,1)}, u32[]{:S(2)}) copy-start(bf16[1024,3072]{1,0:T(8,128)(2,1)} %get-tuple-element.11) | copy-start | bytes 18874372
  213.9 12.1 %copy-start.4 = (bf16[3072,1024]{1,0:T(8,128)(2,1)S(1)}, bf16[3072,1024]{1,0:T(8,128)(2,1)}, u32[]{:S(2)}) copy-start(bf16[3072,1024]{1,0:T(8,128)(2,1)} %get-tuple-element.12) | copy-start | bytes 18874372
  226.0 8.3 %copy-start.1 = (s32[1024]{0:T(1024)S(1)}, s32[1024]{0:T(1024)}, u32[]{:S(2)}) copy-start(s32[1024]{0:T(1024)} %param.20) | copy-start | bytes 12292
  226.1 8.3 %copy-start.2 = (s32[32]{0:T(128)S(1)}, s32[32]{0:T(128)}, u32[]{:S(2)}) copy-start(s32[32]{0:T(128)} %param.21) | copy-start | bytes 388
  226.1 8.4 %copy-start.5 = (bf16[2,512,1024]{2,1,0:T(8,128)(2,1)S(1)}, bf16[2,512,1024]{2,1,0:T(8,128)(2,1)}, u32[]{:S(2)}) copy-start(bf16[2,512,1024]{2,1,0:T(8,128)(2,1)} %param.17) | copy-start | bytes 6291460
  258.4 13.0 %copy-start.6 = (bf16[1024,1024]{1,0:T(8,128)(2,1)S(1)}, bf16[1024,1024]{1,0:T(8,128)(2,1)}, u32[]{:S(2)}) copy-start(bf16[1024,1024]{1,0:T(8,128)(2,1)} %multiply_convert_fusion) | copy-start | bytes 6291460

commit v2 on v1

--- a/solution.py
+++ b/solution.py
@@ -45,40 +45,26 @@
 
 
 def gather_kernel(
-    n_row,
     n_col,
     tok,
     shr,
     dex,
-    gate,
-    up,
-    down,
     tok_o,
     shr_o,
     dex_o,
-    gate_o,
-    up_o,
-    down_o,
     own_sem,
     ring_send,
     ring_recv,
     core_send,
     core_recv,
-    x_send,
-    x_recv,
-    pair_send,
-    pair_recv,
 ):
     row, col = lax.axis_index("row"), lax.axis_index("col")
-    n_x = n_row // 2
-    x, core = row // 2, lax.rem(row, 2)
+    core = lax.rem(row, 2)
     here = ring_position(col, n_col)
     right = (row, ring_col(wrap(here + 1, n_col), n_col))
     left = (row, ring_col(wrap(here - 1, n_col), n_col))
-    twin_row = x * 2 + 1 - core
-    twin = (twin_row, col)
-    x_peers = [(wrap(x + k, n_x) * 2 + core, col) for k in range(1, n_x)]
-    signal_all([left, right, twin] + x_peers)
+    twin = (row + 1 - 2 * core, col)
+    signal_all([left, right, twin])
 
     t_rows, s_rows, e_rows = tok.shape[0], shr.shape[0], dex.shape[0]
     t_half, s_half, e_half = t_rows // 2, s_rows // 4, e_rows // 4
@@ -100,35 +86,6 @@
         if a == 1:
             return rows(shr, core * (s_rows // 2) + d * s_half, s_half)
         return rows(dex, (2 * core + d) * e_half, e_half)
-
-    def weight_place(w, r):
-        if w == 2:
-            width = down.shape[1]
-            return down_o.at[:, pl.ds(pl.multiple_of(r * width, 128), width)]
-        depth = gate.shape[0]
-        return rows((gate_o, up_o)[w], r * depth, depth)
-
-    weights = (gate, up, down)
-
-    def x_copy(w, k, source, place_row):
-        return pltpu.make_async_remote_copy(
-            src_ref=source,
-            dst_ref=weight_place(w, place_row),
-            send_sem=x_send.at[w, k - 1],
-            recv_sem=x_recv.at[w, k - 1],
-            device_id=x_peers[k - 1],
-            device_id_type=MESH,
-        )
-
-    def pair_copy(w, k, source, place_row):
-        return pltpu.make_async_remote_copy(
-            src_ref=source,
-            dst_ref=weight_place(w, place_row),
-            send_sem=pair_send.at[w, k],
-            recv_sem=pair_recv.at[w, k],
-            device_id=twin,
-            device_id_type=MESH,
-        )
 
     def ring_copy(a, d, step, source, block):
         return pltpu.make_async_remote_copy(
@@ -160,9 +117,6 @@
     for a in arrays:
         for d in sides:
             ring_copy(a, d, 0, first(a, d), col).start()
-    for w in range(3):
-        for k in range(1, n_x):
-            x_copy(w, k, weights[w], row).start()
     own = [
         pltpu.make_async_copy(tok, rows(tok_o, col * t_rows, t_rows), own_sem.at[0]),
         pltpu.make_async_copy(dex, rows(dex_o, col * e_rows, e_rows), own_sem.at[1]),
@@ -175,9 +129,6 @@
                 own_sem.at[2 + c],
             )
         )
-    for w in range(3):
-        pair_copy(w, 0, weights[w], row).start()
-        own.append(pltpu.make_async_copy(weights[w], weight_place(w, row), own_sem.at[4 + w]))
     for copy in own:
         copy.start()
 
@@ -194,24 +145,11 @@
                 if a:
                     twin_copy(a, d, step, block, core).start()
 
-    def steps(start, stop):
-        @pl.loop(start, stop)
-        def _(step):
-            ring_step(step, True)
-
-    def pass_on(w):
-        for k in range(1, n_x):
-            source_row = wrap(x - k, n_x) * 2 + core
-            piece = weight_place(w, source_row)
-            x_copy(w, k, piece, source_row).wait_recv()
-            pair_copy(w, k, piece, source_row).start()
-
-    steps(0, last // 2)
-    pass_on(0)
-    steps(last // 2, last)
-    pass_on(1)
+    @pl.loop(0, last)
+    def _(step):
+        ring_step(step, True)
+
     ring_step(last, False)
-    pass_on(2)
 
     @pl.loop(0, last + 1)
     def _(step):
@@ -223,51 +161,36 @@
                     twin_copy(a, d, step, block, core).wait_send()
                     twin_copy(a, d, step, block, 1 - core).wait_recv()
 
-    for w in range(3):
-        for k in range(n_x):
-            if k:
-                x_copy(w, k, weights[w], row).wait_send()
-            source_row = wrap(x - k, n_x) * 2 + core
-            pair_copy(w, k, weight_place(w, source_row), source_row).wait_send()
-            twin_source = wrap(x - k, n_x) * 2 + 1 - core
-            pair_copy(w, k, weight_place(w, twin_source), twin_source).wait_recv()
     for copy in own:
         copy.wait()
 
 
-def gather_all(n_row, n_col, tok, shr, dex, gate, up, down):
+def gather_all(n_col, tok, shr, dex):
     bf = jnp.bfloat16
     outs = [
         (n_col * tok.shape[0], tok.shape[1]),
         (n_col * shr.shape[0], shr.shape[1]),
         (n_col * dex.shape[0], dex.shape[1]),
-        (n_row * gate.shape[0], gate.shape[1]),
-        (n_row * up.shape[0], up.shape[1]),
-        (down.shape[0], n_row * down.shape[1]),
     ]
-    n_x, steps = n_row // 2, n_col - 1
+    steps = n_col - 1
     dma = pltpu.SemaphoreType.DMA
     return pl.pallas_call(
-        functools.partial(gather_kernel, n_row, n_col),
+        functools.partial(gather_kernel, n_col),
         out_shape=[jax.ShapeDtypeStruct(s, bf) for s in outs],
-        in_specs=[pl.BlockSpec(memory_space=pl.ANY)] * 6,
-        out_specs=[pl.BlockSpec(memory_space=pl.ANY)] * 6,
+        in_specs=[pl.BlockSpec(memory_space=pl.ANY)] * 3,
+        out_specs=[pl.BlockSpec(memory_space=pl.ANY)] * 3,
         scratch_shapes=[
-            dma((7,)),
+            dma((4,)),
             dma((3, 2, steps)),
             dma((3, 2, steps)),
             dma((2, 2, steps)),
             dma((2, 2, steps)),
-            dma((3, n_x - 1)),
-            dma((3, n_x - 1)),
-            dma((3, n_x)),
-            dma((3, n_x)),
         ],
         compiler_params=pltpu.CompilerParams(
             collective_id=0, has_side_effects=True, vmem_limit_bytes=VMEM_BYTES
         ),
         name="gather_all",
-    )(tok, shr, dex, gate, up, down)
+    )(tok, shr, dex)
 
 
 def reduce_kernel(n_col, subs, part, out, held, send_sem, recv_sem):
@@ -350,7 +273,6 @@
 
 
 def local(
-    n_row,
     n_col,
     hidden_states,
     norm_gain,
@@ -374,9 +296,10 @@
     by_side = (
         shrink_gu.reshape(owned, 2, rank, -1).transpose(1, 0, 2, 3).reshape(shrink_gu.shape)
     )
-    tokens, shrink, expand_down, gate_full, up_full, down_full = gather_all(
-        n_row, n_col, normed, by_side, down_expand_maps, gate_base, up_base, down_base
-    )
+    gate_full = lax.all_gather(gate_base, "row", axis=0, tiled=True)
+    up_full = lax.all_gather(up_base, "row", axis=0, tiled=True)
+    down_full = lax.all_gather(down_base, "row", axis=1, tiled=True)
+    tokens, shrink, expand_down = gather_all(n_col, normed, by_side, down_expand_maps)
     ranks = adapter_list * rank
     chosen = (jnp.arange(ranks, dtype=jnp.int32) // rank)[None, :] == row_slots[:, None]
 
@@ -414,7 +337,7 @@
     )
     out_specs = P(("row", "col"), None)
     return jax.shard_map(
-        functools.partial(local, mesh.shape["row"], mesh.shape["col"]),
+        functools.partial(local, mesh.shape["col"]),
         mesh=mesh,
         in_specs=in_specs,
         out_specs=out_specs,

time: 351 us -> 270 us (0.77)
  Pallas kernels: 275 us -> 179 us
  between operations: 0.08 us -> 13.2 us
    pallas_call x1, Pallas kernels: 208 us -> 111 us  [gather_all(): pl.pallas_call(functools.partial(gather_kernel, n_col), out_shape=[jax.Sh...]
  transfers between devices with their start and end apart: 0 -> 3, of which waited for: 0 -> 0; matrix products, arithmetic and copies ran while one was open for 0% -> 19% of each run, Pallas kernels for 0% -> 41%
where the time goes in v2:
time: 270 us; the launch traced here: 269 us
  Pallas kernels  179 us (66%)
  matrix products  70.8 us (26%)
  between operations  13.2 us (5%)
  local copies, waits for them, and re-layouts  3.05 us (1%)
    pallas_call x1, Pallas kernels, gather_all(): pl.pallas_call(functools.partial(gather_kernel, n_col), out_shape=[jax.Sh...  111 us
    dot_general x6, matrix products, dot(): return jnp.dot(left, right, preferred_element_type=jnp.float32)  70.8 us
    pallas_call x1, Pallas kernels, reduce_blocks(): pl.pallas_call(functools.partial(reduce_kernel, n_col, subs), out_shape=j...  67.5 us
  transfers between devices with their start and end apart: 3, of which 0 were waited for; matrix products, arithmetic and copies ran while one was open for 19% of the time, Pallas kernels for 41%

profile of v2, /device:TPU:0, one launch (start us, length us, event | category | flops | bytes accessed | tf_op | source)
XLA Modules:
  0.0 269.5 jit_solution(7188922662901769513)
XLA Ops:
  6.5 0.0 copy-start
  6.5 0.0 copy-start.2
  6.5 0.0 copy-start.1
  6.5 0.0 copy-start.3
  6.5 0.0 all-gather.6.cloned.1.call-start
  6.6 0.7 all-gather.6.cloned.1.call-update
  7.3 0.0 copy-start.4
  7.3 0.0 copy-start.5
  7.3 0.0 all-gather.4.cloned.1.call-start
  7.3 0.7 all-gather.4.cloned.1.call-update
  8.0 0.0 all-gather.8.cloned.1.call-start
  8.1 0.7 all-gather.8.cloned.1.call-update
  8.8 0.0 copy-done.2
  8.8 1.0 copy.13
  9.8 0.0 copy-done.1
  9.8 0.2 fusion.11
  10.0 0.0 copy-done.3
  10.0 1.1 fusion.13.tok
  11.2 111.2 %gather_all.1 = (bf16[1024,3072]{1,0:T(8,128)(2,1)}, bf16[1024,3072]{1,0:T(8,128)(2,1)}, bf16[512,3072]{1,0:T(8,128)(2,1)}) custom-call(bf16[128,3072]{1,0:T(8,128)(2,1)} %fusion.13.tok, bf16[128,3072]{1,0:T(8,128)(2,1)} %bitcast.21, bf16[64,3072]{1,0:T(8,128)(2,1)} %dex.1), custom_call_target="tpu_custom_call" | custom-call | tf_op jit(solution)/shard_map/gather_all/pallas_call | solution.py:177
  122.4 0.0 copy-done.4
  122.4 0.0 copy-done.5
  122.4 0.1 select_reduce_fusion
  122.5 10.5 %fusion.17 = f32[1024,1024]{1,0:T(8,128)} fusion(bf16[2,512,1024]{2,1,0:T(8,128)(2,1)} %param.17, bf16[1024,3072]{1,0:T(8,128)(2,1)} %get-tuple-element.8, bf16[1024,3072]{1,0:T(8,128)(2,1)} %get-tuple-element.9, s32[512]{0:T(512)S(1)} %add_select_fusion, s32[1024]{0:T(1024)S(1)} %select_reduce_fusion), kind=kOutput, calls=%fused_computation.18 | convolution fusion | flops 4296540160 | bytes 14686208 | tf_op jit(solution)/shard_map/dot_general | solution.py:310
  133.0 0.0 all-gather.6.cloned.1.call-done
  133.0 11.9 %fusion.33 = f32[1024,1024]{1,0:T(8,128)} fusion(bf16[1024,3072]{1,0:T(8,128)(2,1)} %get-tuple-element.8, bf16[3072,1024]{1,0:T(8,128)(2,1)} %all-gather.6.cloned.1.call-done), kind=kOutput, calls=%fused_computation.39 | convolution fusion | flops 6442450944 | bytes 16777216 | tf_op jit(solution)/shard_map/dot_general | solution.py:310
  144.9 0.0 all-gather.4.cloned.1.call-done
  144.9 12.0 %fusion.32 = f32[1024,1024]{1,0:T(8,128)} fusion(bf16[1024,3072]{1,0:T(8,128)(2,1)} %get-tuple-element.8, bf16[3072,1024]{1,0:T(8,128)(2,1)} %all-gather.4.cloned.1.call-done), kind=kOutput, calls=%fused_computation.38 | convolution fusion | flops 6442450944 | bytes 16777216 | tf_op jit(solution)/shard_map/dot_general | solution.py:310
  156.9 13.9 %multiply_convert_fusion = bf16[1024,1024]{1,0:T(8,128)(2,1)} fusion(f32[1024,1024]{1,0:T(8,128)} %fusion.33, f32[1024,1024]{1,0:T(8,128)} %fusion.32, f32[1024,1024]{1,0:T(8,128)} %fusion.17, bf16[1024,3072]{1,0:T(8,128)(2,1)} %get-tuple-element.8, bf16[1024,3072]{1,0:T(8,128)(2,1)} %get-tuple-element.9, bf16[2,512,1024]{2,1,0:T(8,128)(2,1)} %param.17, ...), kind=kOutput, calls=%fused_computation.1 | convolution fusion | flops 4304928768 | bytes 25171968 | tf_op jit(solution)/shard_map/dot_general | solution.py:310
  170.8 0.0 all-gather.8.cloned.1.call-done
  170.8 12.0 %fusion.34 = f32[1024,3072]{1,0:T(8,128)} fusion(bf16[1024,1024]{1,0:T(8,128)(2,1)} %multiply_convert_fusion, bf16[1024,3072]{1,0:T(8,128)(2,1)} %all-gather.8.cloned.1.call-done), kind=kOutput, calls=%fused_computation.40 | convolution fusion | flops 6442450944 | bytes 20971520 | tf_op jit(solution)/shard_map/dot_general | solution.py:310
  182.8 0.0 copy-done
  182.8 10.6 %add_convert_fusion.part = bf16[1024,3072]{1,0:T(8,128)(2,1)} fusion(f32[1024,3072]{1,0:T(8,128)} %fusion.34, bf16[512,3072]{1,0:T(8,128)(2,1)} %get-tuple-element.10, bf16[1024,1024]{1,0:T(8,128)(2,1)} %multiply_convert_fusion, bf16[512,1024]{1,0:T(8,128)(2,1)S(1)} %copy-done, s32[512]{0:T(512)S(1)} %add_select_fusion, s32[1024]{0:T(1024)S(1)} %select_reduce_fusion), kind=kOutput, calls=%fused_computation | convolution fusion | flops 4302831616 | bytes 25171968 | tf_op jit(solution)/shard_map/dot_general | solution.py:310
  193.3 67.5 %reduce_blocks.1 = bf16[128,3072]{1,0:T(8,128)(2,1)} custom-call(bf16[1024,3072]{1,0:T(8,128)(2,1)} %add_convert_fusion.part), custom_call_target="tpu_custom_call" | custom-call | tf_op jit(solution)/shard_map/reduce_blocks/pallas_call | solution.py:258
  260.9 2.1 copy.15
  (2 shorter events, 0.0 us)
Async XLA Ops:
  6.5 176.3 %copy-start = (bf16[512,1024]{1,0:T(8,128)(2,1)S(1)}, bf16[512,1024]{1,0:T(8,128)(2,1)}, u32[]{:S(2)}) copy-start(bf16[512,1024]{1,0:T(8,128)(2,1)} %param.18) | copy-start | bytes 3145732
  6.5 2.2 copy-start.2
  6.5 3.2 %copy-start.1 = (bf16[128,3072]{1,0:T(8,128)(2,1)S(1)}, bf16[128,3072]{1,0:T(8,128)(2,1)}, u32[]{:S(2)}) copy-start(bf16[128,3072]{1,0:T(8,128)(2,1)} %param.11) | copy-start | bytes 2359300
  6.5 3.5 %copy-start.3 = (f32[3072]{0:T(1024)S(1)}, f32[3072]{0:T(1024)}, u32[]{:S(2)}) copy-start(f32[3072]{0:T(1024)} %param.12) | copy-start | bytes 36868
  6.5 126.5 %all-gather.6.cloned.1.call-start = ((), (), s32[]{:S(2)}) async-start(), calls=%async_computation.1 | async-start | bytes 7864320 | tf_op jit(solution)/shard_map/all_gather | solution.py:300
  7.3 115.1 %copy-start.4 = (s32[1024]{0:T(1024)S(1)}, s32[1024]{0:T(1024)}, u32[]{:S(2)}) copy-start(s32[1024]{0:T(1024)} %param.20) | copy-start | bytes 12292
  7.3 115.1 %copy-start.5 = (s32[32]{0:T(128)S(1)}, s32[32]{0:T(128)}, u32[]{:S(2)}) copy-start(s32[32]{0:T(128)} %param.21) | copy-start | bytes 388
  7.3 137.6 %all-gather.4.cloned.1.call-start = ((), (), s32[]{:S(2)}) async-start(), calls=%async_computation | async-start | bytes 7864320 | tf_op jit(solution)/shard_map/all_gather | solution.py:299
  8.0 162.8 %all-gather.8.cloned.1.call-start = ((), (), s32[]{:S(2)}) async-start(), calls=%async_computation.2 | async-start | bytes 7864320 | tf_op jit(solution)/shard_map/all_gather | solution.py:301
Sparse Core Ops, SparseCore 0:
  8.9 49.0 all-gather.5
  59.6 46.3 all-gather.3
  107.6 46.3 all-gather.7
